TPU v7x, 32 devices: a whole 2x2x4 slice. The times are simulated.
32 devices in a mesh: section: 2 (over core), dp: 16 (over z, y, x).
Axes of the slice: x: 2, y: 2, z: 4, core: 2. Of those that a mesh axis runs over, the one named last changes fastest.
Arguments:
- inputs: bfloat16 [2, 1, 128, 128, 512], P(None, None, 'dp'), may hold values from -64 to 64
- cotangent: bfloat16 [2, 1, 128, 128, 512], P(None, None, 'dp'), may hold values from -6 to 6
- shapes: int32 [2, 2], replicated, may hold values from 96 to 128, as said below
- local_to_local: bfloat16 [2, 2, 9, 128, 128], P('section'), may hold values from -0.09375 to 0.09375
- global_to_local: bfloat16 [2, 2, 9, 384, 128], P('section'), may hold values from -0.09375 to 0.09375
- local_to_global: bfloat16 [2, 2, 9, 128, 384], P('section'), may hold values from -0.1875 to 0.1875
- spec_reduce: bfloat16 [2, 2, 384, 192], P('section'), may hold values from -0.3125 to 0.3125
- spec_mix: bfloat16 [2, 2, 384, 384], P('section'), may hold values from -0.3125 to 0.3125
- spec_expand: bfloat16 [2, 2, 192, 384], P('section'), may hold values from -0.4375 to 0.4375
- norm_gains: float32 [2, 2, 1088], P('section'), may hold values from 0.1 to 1.9
- norm_biases: float32 [2, 2, 1088], P('section'), may hold values from -3 to 3
- run_means: float32 [2, 2, 1088], P('section'), may hold values from -3 to 3
- run_vars: float32 [2, 2, 1088], P('section'), may hold values from 0.5 to 2
Outputs:
- block_outputs: bfloat16 [2, 2, 1, 128, 128, 512], P('section', None, None, 'dp')
- input_grads: float32 [2, 2, 1, 128, 128, 512], P('section', None, None, 'dp')
- grad_local_to_local: float32 [2, 2, 9, 128, 128], P('section')
- grad_global_to_local: float32 [2, 2, 9, 384, 128], P('section')
- grad_local_to_global: float32 [2, 2, 9, 128, 384], P('section')
- grad_spec_reduce: float32 [2, 2, 384, 192], P('section')
- grad_spec_mix: float32 [2, 2, 384, 384], P('section')
- grad_spec_expand: float32 [2, 2, 192, 384], P('section')
- grad_gains: float32 [2, 2, 1088], P('section')
- grad_biases: float32 [2, 2, 1088], P('section')
- new_means: float32 [2, 2, 1088], P('section')
- new_vars: float32 [2, 2, 1088], P('section')
Inputs may be any that keep to these rules, and one draw needn't show every extreme that they name: `shapes`: each row is (height, width) of all maps of a micro-batch, both multiples of 8; some micro-batch has height 128.
All inputs are finite; a program needn't handle non-finite values.
Results may differ from a plain program's by a relative error of at most 0.025.
Values may be sent and summed in bfloat16 or wider, within the bound.
A program may use at most 256 MiB of HBM per device.

v0:
```python
import jax
import jax.numpy as jnp
from jax import lax
from jax.experimental import pallas as pl
from jax.experimental.pallas import tpu as pltpu
from jax.sharding import PartitionSpec as P

CL = 128
CG = 384
CS = 192
LONG = 128


EPSILON = 1e-05
MOMENTUM = 0.1
PRECISE = lax.Precision.HIGHEST


def with_halo(block, sides, width):
    for axis, dim in sides:
        count = lax.axis_size(axis)
        forward = [(i, i + 1) for i in range(count - 1)]
        backward = [(target, source) for source, target in forward]
        low = lax.ppermute(
            lax.slice_in_dim(block, block.shape[dim] - width, None, axis=dim), axis, forward
        )
        high = lax.ppermute(lax.slice_in_dim(block, 0, width, axis=dim), axis, backward)
        block = jnp.concatenate([low, block, high], axis=dim)
    return block


def from_behind(value, axis, steps):
    count = lax.axis_size(axis)
    first, last = (max(0, -steps), min(count, count - steps))
    return lax.ppermute(value, axis, [(source, source + steps) for source in range(first, last)])


def dft_tables(height, width, long_side, freq_total):
    position = jnp.arange(long_side, dtype=jnp.int32)
    frequency = jnp.arange(freq_total, dtype=jnp.int32)
    half_width = width // 2
    width_real = width.astype(jnp.float32)
    height_real = height.astype(jnp.float32)
    width_phase = position[:, None] * frequency[None, :] % width
    width_angle = 2.0 * jnp.pi / width_real * width_phase.astype(jnp.float32)
    width_valid = ((position[:, None] < width) & (frequency[None, :] <= half_width)).astype(
        jnp.float32
    )
    width_scale = lax.rsqrt(width_real)
    fwd_cos = jnp.cos(width_angle) * width_scale * width_valid
    fwd_sin = -jnp.sin(width_angle) * width_scale * width_valid
    edge_freq = (frequency == 0) | (frequency == half_width)
    freq_weight = jnp.where(edge_freq, 1.0, 2.0).astype(jnp.float32)
    inv_cos = freq_weight[:, None] * fwd_cos.T
    inv_sin = freq_weight[:, None] * fwd_sin.T
    height_phase = position[:, None] * position[None, :] % height
    height_angle = 2.0 * jnp.pi / height_real * height_phase.astype(jnp.float32)
    height_valid = ((position[:, None] < height) & (position[None, :] < height)).astype(jnp.float32)
    height_scale = lax.rsqrt(height_real)
    row_cos = jnp.cos(height_angle) * height_scale * height_valid
    row_sin = jnp.sin(height_angle) * height_scale * height_valid
    return (fwd_cos, fwd_sin, inv_cos, inv_sin, row_cos, row_sin)


def geometry(shape_row, band_index, band_size, freq_total, freq_local, map_count):
    height = shape_row[0]
    width = shape_row[1]
    position = jnp.arange(LONG, dtype=jnp.int32)
    band_rows = band_index * band_size + jnp.arange(band_size, dtype=jnp.int32)
    pix_mask = ((band_rows[:, None] < height) & (position[None, :] < width)).astype(jnp.float32)[
        None, :, :, None
    ]
    local_freq = band_index * freq_local + jnp.arange(freq_local, dtype=jnp.int32)
    freq_mask = ((position[:, None] < height) & (local_freq[None, :] <= width // 2)).astype(
        jnp.float32
    )[None, :, :, None]
    pix_count = (map_count * height * width).astype(jnp.float32)
    spec_count = (map_count * height * (width // 2 + 1)).astype(jnp.float32)
    return (pix_mask, freq_mask, pix_count, spec_count, dft_tables(height, width, LONG, freq_total))


def conv_rows(padded, kernel):
    shaped = kernel.reshape(3, 3, kernel.shape[1], kernel.shape[2])
    return lax.conv_general_dilated(
        padded,
        shaped,
        (1, 1),
        "VALID",
        dimension_numbers=("NHWC", "HWIO", "NHWC"),
        preferred_element_type=jnp.float32,
    )


def flipped(kernel):
    shaped = kernel.reshape(3, 3, kernel.shape[1], kernel.shape[2])[::-1, ::-1]
    return jnp.swapaxes(shaped, 2, 3).reshape(9, kernel.shape[2], kernel.shape[1])


def kernel_grad(padded, grad_out, band_size, width):
    tap_grads = []
    for row_tap in range(3):
        for col_tap in range(3):
            window = padded[:, row_tap : row_tap + band_size, col_tap : col_tap + width, :]
            tap_grads.append(
                jnp.einsum("mrwi,mrwo->io", window, grad_out, preferred_element_type=jnp.float32)
            )
    return jnp.stack(tap_grads)


def width_forward(entry, table):
    return jnp.einsum("mrwc,wf->mrfc", entry, table, precision=PRECISE)


def width_forward_adj(entry, table):
    return jnp.einsum("mrfc,wf->mrwc", entry, table, precision=PRECISE)


def width_inverse(entry, table):
    return jnp.einsum("mrfc,fw->mrwc", entry, table, precision=PRECISE)


def width_inverse_adj(entry, table):
    return jnp.einsum("mrwc,fw->mrfc", entry, table, precision=PRECISE)


def height_apply(table, entry):
    return jnp.einsum("kn,mnfc->mkfc", table, entry, precision=PRECISE)


def height_adjoint(table, entry):
    return jnp.einsum("kn,mkfc->mnfc", table, entry, precision=PRECISE)


def rows_forward(row_cos, row_sin, entry):
    half_ch = entry.shape[-1] // 2
    real_in = entry[..., :half_ch]
    imag_in = entry[..., half_ch:]
    real_out = height_apply(row_cos, real_in) + height_apply(row_sin, imag_in)
    imag_out = height_apply(row_cos, imag_in) - height_apply(row_sin, real_in)
    return jnp.concatenate([real_out, imag_out], axis=-1)


def rows_inverse(row_cos, row_sin, entry):
    half_ch = entry.shape[-1] // 2
    real_in = entry[..., :half_ch]
    imag_in = entry[..., half_ch:]
    real_out = height_adjoint(row_cos, real_in) - height_adjoint(row_sin, imag_in)
    imag_out = height_adjoint(row_cos, imag_in) + height_adjoint(row_sin, real_in)
    return jnp.concatenate([real_out, imag_out], axis=-1)


def split_pairs(totals, widths):
    pairs = []
    offset = 0
    for lead_width, tail_width in zip(widths[0::2], widths[1::2]):
        lead_part = totals[offset : offset + lead_width]
        tail_part = totals[offset + lead_width : offset + lead_width + tail_width]
        pairs.append((lead_part, tail_part))
        offset = offset + lead_width + tail_width
    return pairs


def moments(entries, weights):
    pieces = []
    for entry, weight in zip(entries, weights):
        masked = entry * weight
        pieces.append(jnp.sum(masked, axis=(0, 1, 2)))
        pieces.append(jnp.sum(masked * entry, axis=(0, 1, 2)))
    totals = lax.psum(jnp.concatenate(pieces), "dp")
    return split_pairs(totals, [piece.shape[0] for piece in pieces])


def grad_moments(grads_in, normed_in):
    pieces = []
    for grad_pre, normed in zip(grads_in, normed_in):
        pieces.append(jnp.sum(grad_pre, axis=(0, 1, 2)))
        pieces.append(jnp.sum(grad_pre * normed, axis=(0, 1, 2)))
    totals = lax.psum(jnp.concatenate(pieces), "dp")
    return split_pairs(totals, [piece.shape[0] for piece in pieces])


def normalize(entry, sum_pair, count_now):
    mean_val = sum_pair[0] / count_now
    var_val = sum_pair[1] / count_now - mean_val * mean_val
    inv_std = lax.rsqrt(var_val + EPSILON)
    return ((entry - mean_val) * inv_std, inv_std, mean_val, var_val)


def silu_slope(pre_act):
    sigmoid_val = jax.nn.sigmoid(pre_act)
    return sigmoid_val * (1.0 + pre_act * (1.0 - sigmoid_val))


def norm_backward(grad_pre, normed, inv_std, gain_part, sum_pair, count_now, weight):
    return (
        weight
        * inv_std
        * gain_part
        * (grad_pre - sum_pair[0] / count_now - normed * sum_pair[1] / count_now)
    )


def layer_forward(layer_in, geometry_now, kernels, gain_vec, bias_vec):
    pix_mask, freq_mask, pix_count, spec_count, tables = geometry_now
    fwd_cos, fwd_sin, inv_cos, inv_sin, row_cos, row_sin = tables
    local_kernel, lift_kernel, reduce_kernel, mix_kernel, expand_kernel = kernels
    acts_low = layer_in.astype(jnp.bfloat16)
    padded = with_halo(acts_low, (("dp", 1),), 1)
    padded = jnp.pad(padded, ((0, 0), (0, 0), (1, 1), (0, 0)))
    local_out = conv_rows(padded, local_kernel)
    global_conv = conv_rows(padded[..., :CL], lift_kernel)
    reduced = jnp.einsum(
        "mrwc,cd->mrwd", acts_low[..., CL:], reduce_kernel, preferred_element_type=jnp.float32
    )
    one_stats = moments([reduced], [pix_mask])[0]
    normed_one, inv_one, mean_one, var_one = normalize(reduced, one_stats, pix_count)
    pre_one = normed_one * gain_vec[:CS] + bias_vec[:CS]
    upper_spec = jax.nn.silu(pre_one) * pix_mask
    spectrum = jnp.concatenate(
        [width_forward(upper_spec, fwd_cos), width_forward(upper_spec, fwd_sin)], axis=-1
    ).astype(jnp.bfloat16)
    columns = lax.all_to_all(spectrum, "dp", split_axis=2, concat_axis=1, tiled=True).astype(
        jnp.float32
    )
    spectra = rows_forward(row_cos, row_sin, columns).astype(jnp.bfloat16)
    mixed = jnp.einsum("mkfc,cd->mkfd", spectra, mix_kernel, preferred_element_type=jnp.float32)
    two_stats = moments([mixed], [freq_mask])[0]
    normed_two, inv_two, mean_two, var_two = normalize(mixed, two_stats, spec_count)
    pre_two = normed_two * gain_vec[CS : 3 * CS] + bias_vec[CS : 3 * CS]
    activated = jax.nn.silu(pre_two) * freq_mask
    inverse = rows_inverse(row_cos, row_sin, activated).astype(jnp.bfloat16)
    returned = lax.all_to_all(inverse, "dp", split_axis=1, concat_axis=2, tiled=True).astype(
        jnp.float32
    )
    half_ch = returned.shape[-1] // 2
    restored = width_inverse(returned[..., :half_ch], inv_cos) + width_inverse(
        returned[..., half_ch:], inv_sin
    )
    summed = (upper_spec + restored).astype(jnp.bfloat16)
    spec_out = jnp.einsum(
        "mrwc,cd->mrwd", summed, expand_kernel, preferred_element_type=jnp.float32
    )
    global_out = global_conv + spec_out
    loc_stats, glo_stats = moments([local_out, global_out], [pix_mask, pix_mask])
    normed_loc, inv_loc, mean_loc, var_loc = normalize(local_out, loc_stats, pix_count)
    normed_glo, inv_glo, mean_glo, var_glo = normalize(global_out, glo_stats, pix_count)
    pre_loc = normed_loc * gain_vec[3 * CS : 3 * CS + CL] + bias_vec[3 * CS : 3 * CS + CL]
    pre_glo = normed_glo * gain_vec[3 * CS + CL :] + bias_vec[3 * CS + CL :]
    result = jnp.concatenate([jax.nn.silu(pre_loc), jax.nn.silu(pre_glo)], axis=-1) * pix_mask
    stored = (
        padded,
        pre_one,
        normed_one,
        inv_one,
        spectra,
        pre_two,
        normed_two,
        inv_two,
        summed,
        pre_loc,
        normed_loc,
        inv_loc,
        pre_glo,
        normed_glo,
        inv_glo,
    )
    means_layer = jnp.concatenate([mean_one, mean_two, mean_loc, mean_glo])
    vars_layer = jnp.concatenate([var_one, var_two, var_loc, var_glo])
    return (result, stored, (means_layer, vars_layer))


def layer_backward(grad_result, stored, geometry_now, kernels, gain_vec):
    (
        padded,
        pre_one,
        normed_one,
        inv_one,
        spectra,
        pre_two,
        normed_two,
        inv_two,
        summed,
        pre_loc,
        normed_loc,
        inv_loc,
        pre_glo,
        normed_glo,
        inv_glo,
    ) = stored
    pix_mask, freq_mask, pix_count, spec_count, tables = geometry_now
    fwd_cos, fwd_sin, inv_cos, inv_sin, row_cos, row_sin = tables
    local_kernel, lift_kernel, reduce_kernel, mix_kernel, expand_kernel = kernels
    band_size = pre_one.shape[1]
    width = pre_one.shape[2]
    grad_loc = grad_result[..., :CL] * pix_mask * silu_slope(pre_loc)
    grad_glo = grad_result[..., CL:] * pix_mask * silu_slope(pre_glo)
    loc_pair, glo_pair = grad_moments([grad_loc, grad_glo], [normed_loc, normed_glo])
    d_local = norm_backward(
        grad_loc, normed_loc, inv_loc, gain_vec[3 * CS : 3 * CS + CL], loc_pair, pix_count, pix_mask
    ).astype(jnp.bfloat16)
    d_global = norm_backward(
        grad_glo, normed_glo, inv_glo, gain_vec[3 * CS + CL :], glo_pair, pix_count, pix_mask
    ).astype(jnp.bfloat16)
    grad_expand = jnp.einsum("mrwc,mrwd->cd", summed, d_global, preferred_element_type=jnp.float32)
    d_summed = jnp.einsum(
        "mrwd,cd->mrwc", d_global, expand_kernel, preferred_element_type=jnp.float32
    )
    d_returned = jnp.concatenate(
        [width_inverse_adj(d_summed, inv_cos), width_inverse_adj(d_summed, inv_sin)], axis=-1
    ).astype(jnp.bfloat16)
    d_inverse = lax.all_to_all(d_returned, "dp", split_axis=2, concat_axis=1, tiled=True).astype(
        jnp.float32
    )
    d_activated = rows_forward(row_cos, row_sin, d_inverse)
    grad_two = d_activated * freq_mask * silu_slope(pre_two)
    two_pair = grad_moments([grad_two], [normed_two])[0]
    d_mixed = norm_backward(
        grad_two, normed_two, inv_two, gain_vec[CS : 3 * CS], two_pair, spec_count, freq_mask
    ).astype(jnp.bfloat16)
    grad_mix = jnp.einsum("mkfc,mkfd->cd", spectra, d_mixed, preferred_element_type=jnp.float32)
    d_spectra = jnp.einsum("mkfd,cd->mkfc", d_mixed, mix_kernel, preferred_element_type=jnp.float32)
    d_columns = rows_inverse(row_cos, row_sin, d_spectra).astype(jnp.bfloat16)
    d_spectrum = lax.all_to_all(d_columns, "dp", split_axis=1, concat_axis=2, tiled=True).astype(
        jnp.float32
    )
    half_ch = d_spectrum.shape[-1] // 2
    d_upper = (
        d_summed
        + width_forward_adj(d_spectrum[..., :half_ch], fwd_cos)
        + width_forward_adj(d_spectrum[..., half_ch:], fwd_sin)
    )
    grad_one = d_upper * pix_mask * silu_slope(pre_one)
    one_pair = grad_moments([grad_one], [normed_one])[0]
    d_reduced = norm_backward(
        grad_one, normed_one, inv_one, gain_vec[:CS], one_pair, pix_count, pix_mask
    ).astype(jnp.bfloat16)
    acts_low = padded[:, 1:-1, 1:-1, :]
    grad_reduce = jnp.einsum(
        "mrwc,mrwd->cd", acts_low[..., CL:], d_reduced, preferred_element_type=jnp.float32
    )
    d_global_in = jnp.einsum(
        "mrwd,cd->mrwc", d_reduced, reduce_kernel, preferred_element_type=jnp.float32
    )
    grad_outs = jnp.concatenate([d_local, d_global], axis=-1)
    grad_pad = with_halo(grad_outs, (("dp", 1),), 1)
    grad_pad = jnp.pad(grad_pad, ((0, 0), (0, 0), (1, 1), (0, 0)))
    d_acts = conv_rows(grad_pad[..., :CL], flipped(local_kernel))
    d_lift = conv_rows(grad_pad[..., CL:], flipped(lift_kernel))
    d_input = d_acts + jnp.concatenate([d_lift, d_global_in], axis=-1)
    grad_local_kernel = kernel_grad(padded, d_local, band_size, width)
    grad_lift = kernel_grad(padded[..., :CL], d_global, band_size, width)
    gains_grad = jnp.concatenate([one_pair[1], two_pair[1], loc_pair[1], glo_pair[1]])
    biases_grad = jnp.concatenate([one_pair[0], two_pair[0], loc_pair[0], glo_pair[0]])
    return (
        d_input,
        (grad_local_kernel, grad_lift, grad_reduce, grad_mix, grad_expand),
        (gains_grad, biases_grad),
    )


def block_forward(block_in, geometry_now, kernels, gain_all, bias_all):
    base = block_in.astype(jnp.float32) * geometry_now[0]
    first_out, first_stored, first_stats = layer_forward(
        base, geometry_now, kernels[0], gain_all[0], bias_all[0]
    )
    second_out, second_stored, second_stats = layer_forward(
        first_out, geometry_now, kernels[1], gain_all[1], bias_all[1]
    )
    return (
        (second_out + base).astype(jnp.bfloat16),
        (first_stored, second_stored),
        (first_stats, second_stats),
    )


def block_backward(grad_in, stored, geometry_now, kernels, gain_all):
    pix_mask = geometry_now[0]
    grad_masked = grad_in * pix_mask
    d_first, second_kernels, second_norms = layer_backward(
        grad_masked, stored[1], geometry_now, kernels[1], gain_all[1]
    )
    d_base, first_kernels, first_norms = layer_backward(
        d_first, stored[0], geometry_now, kernels[0], gain_all[0]
    )
    return (
        (grad_masked + d_base) * pix_mask,
        (first_kernels, second_kernels),
        (first_norms, second_norms),
    )


def running_update(mean_now, var_now, layer_stats, geometry_now):
    pix_count = geometry_now[2]
    spec_count = geometry_now[3]
    counts = jnp.concatenate(
        [
            jnp.full((CS,), pix_count, jnp.float32),
            jnp.full((2 * CS,), spec_count, jnp.float32),
            jnp.full((CL + CG,), pix_count, jnp.float32),
        ]
    )
    batch_means = jnp.stack([layer_stats[0][0], layer_stats[1][0]])
    batch_vars = jnp.stack([layer_stats[0][1], layer_stats[1][1]])
    new_mean = (1.0 - MOMENTUM) * mean_now + MOMENTUM * batch_means
    new_var = (1.0 - MOMENTUM) * var_now + MOMENTUM * batch_vars * counts / (counts - 1.0)
    return (new_mean, new_var)


def on_device(
    inputs,
    cotangent,
    shapes,
    local_to_local,
    global_to_local,
    local_to_global,
    spec_reduce,
    spec_mix,
    spec_expand,
    norm_gains,
    norm_biases,
    run_means,
    run_vars,
):
    section_id = lax.axis_index("section")
    band_index = lax.axis_index("dp")
    n_dp = lax.axis_size("dp")
    micro_count = inputs.shape[0]
    map_count = inputs.shape[1]
    band_size = inputs.shape[2]
    freq_total = (LONG // 2 + n_dp) // n_dp * n_dp
    freq_local = freq_total // n_dp
    kernels = []
    for layer_pos in range(2):
        local_kernel = jnp.concatenate(
            [local_to_local[0, layer_pos], global_to_local[0, layer_pos]], axis=1
        )
        kernels.append(
            (
                local_kernel,
                local_to_global[0, layer_pos],
                spec_reduce[0, layer_pos],
                spec_mix[0, layer_pos],
                spec_expand[0, layer_pos],
            )
        )
    gain_all = norm_gains[0]
    bias_all = norm_biases[0]
    received = jnp.zeros(inputs.shape[1:], jnp.bfloat16)
    run_mean = run_means[0]
    run_var = run_vars[0]
    outputs = jnp.zeros(inputs.shape, jnp.bfloat16)
    saved_inputs = []
    saved_geometry = []
    for tick_pos in range(micro_count + 1):
        micro_index = tick_pos - section_id
        is_valid = (micro_index >= 0) & (micro_index < micro_count)
        micro_slot = jnp.clip(micro_index, 0, micro_count - 1)
        own_input = lax.dynamic_index_in_dim(inputs, micro_slot, 0, keepdims=False)
        block_in = jnp.where(section_id == 0, own_input, received)
        shape_row = lax.dynamic_index_in_dim(shapes, micro_slot, 0, keepdims=False)
        geometry_now = geometry(shape_row, band_index, band_size, freq_total, freq_local, map_count)
        block_out, stored, layer_stats = block_forward(
            block_in, geometry_now, kernels, gain_all, bias_all
        )
        new_mean, new_var = running_update(run_mean, run_var, layer_stats, geometry_now)
        run_mean = jnp.where(is_valid, new_mean, run_mean)
        run_var = jnp.where(is_valid, new_var, run_var)
        updated = lax.dynamic_update_index_in_dim(outputs, block_out, micro_slot, 0)
        outputs = jnp.where(is_valid, updated, outputs)
        saved_inputs.append(block_in)
        saved_geometry.append(geometry_now)
        if tick_pos < micro_count:
            received = from_behind(block_out, "section", 1)
    kernel_acc = [jnp.zeros((2,) + part_now.shape, jnp.float32) for part_now in kernels[0]]
    gain_acc = jnp.zeros(gain_all.shape, jnp.float32)
    bias_acc = jnp.zeros(bias_all.shape, jnp.float32)
    received_grad = jnp.zeros(inputs.shape[1:], jnp.bfloat16)
    grads_out = jnp.zeros(inputs.shape, jnp.float32)
    for tick_pos in range(micro_count + 1):
        micro_index = micro_count - tick_pos - section_id
        is_valid = (micro_index >= 0) & (micro_index < micro_count)
        micro_slot = jnp.clip(micro_index, 0, micro_count - 1)
        scale_valid = is_valid.astype(jnp.float32)
        forward_tick = micro_count - tick_pos
        geometry_now = saved_geometry[forward_tick]
        recomputed = block_forward(
            saved_inputs[forward_tick], geometry_now, kernels, gain_all, bias_all
        )
        stored = recomputed[1]
        own_grad = lax.dynamic_index_in_dim(cotangent, micro_slot, 0, keepdims=False)
        grad_in = jnp.where(section_id == 1, own_grad, received_grad).astype(jnp.float32)
        grad_input, kernel_grads, norm_grads = block_backward(
            grad_in, stored, geometry_now, kernels, gain_all
        )
        sent_grad = grad_input.astype(jnp.bfloat16)
        kept_grad = jnp.where(section_id == 1, sent_grad.astype(jnp.float32), grad_input)
        updated = lax.dynamic_update_index_in_dim(grads_out, kept_grad, micro_slot, 0)
        grads_out = jnp.where(is_valid, updated, grads_out)
        stacked = [
            jnp.stack([kernel_grads[0][part_pos], kernel_grads[1][part_pos]]) * scale_valid
            for part_pos in range(5)
        ]
        gain_acc = gain_acc + jnp.stack([norm_grads[0][0], norm_grads[1][0]]) * scale_valid
        bias_acc = bias_acc + jnp.stack([norm_grads[0][1], norm_grads[1][1]]) * scale_valid
        kernel_acc = [acc_part + new_part for acc_part, new_part in zip(kernel_acc, stacked)]
        if tick_pos < micro_count:
            received_grad = from_behind(sent_grad, "section", -1)
    totals = lax.psum(
        (kernel_acc[0], kernel_acc[1], kernel_acc[2], kernel_acc[3], kernel_acc[4]), "dp"
    )
    grad_ll = totals[0][:, :, :CL, :]
    grad_gl = totals[0][:, :, CL:, :]
    return (
        outputs[None],
        grads_out[None],
        grad_ll[None],
        grad_gl[None],
        totals[1][None],
        totals[2][None],
        totals[3][None],
        totals[4][None],
        gain_acc[None],
        bias_acc[None],
        run_mean[None],
        run_var[None],
    )


F32 = jnp.float32
BF16 = jnp.bfloat16
MESH = pl.DeviceIdType.MESH
MEMBERS = 16
ROWS = 8
LAYERS = 4
PAIRS = 4
HALF = 192
FULL = 384
SLOTS = 640
PIECES = 32
EARLY = 272
LATE = 64
AT_LL = 0
AT_GL = 1152
AT_KG = 4608
AT_E = 8064
AT_M = 0
AT_R = 1152
SECTION_NAMES = ("one", "two", "out")


def dot(a, b):
    return lax.dot_general(a, b, (((1,), (0,)), ((), ())), preferred_element_type=F32)


def dot_nt(a, b):
    return lax.dot_general(a, b, (((1,), (1,)), ((), ())), preferred_element_type=F32)


def dot_tn(a, b):
    return lax.dot_general(a, b, (((0,), (0,)), ((), ())), preferred_element_type=F32)


def sigmoid(v):
    return 0.5 * jnp.tanh(0.5 * v) + 0.5


def fold(v):
    return jnp.sum(v.reshape(v.shape[0] // 8, 8, v.shape[1]), axis=0)


def wide(row, lanes):
    whole, rest = divmod(lanes, 128)
    parts = [row] * whole + ([row[:, :rest]] if rest else [])
    return jnp.concatenate(parts, axis=1)


def network_kernel(
    inputs, cot, shapes, ll, gl, lg, red, mix, exp, gains, biases, run_m, run_v,
    out_y, out_g, out_we, out_wl, out_gains, out_biases, out_m, out_v,
    w_c, w_gl, w_r, w_m, w_e, raw_g, raw_b, pars, acts, shifted, halo, v1, u, spec, mixed, tsum, v34,
    pmask, qmask, tf, tft, tg, tgt, hf, hi, vab, e2, dq, ds, g, gblk, at,
    gwe, gwl, rbe, rbl, fine, finl,
    ssum, rsum, send, recv, stats, stats_far,
    sem_w, sem_in, sem_cot, sem_halo_s, sem_halo_r, sem_ar_s, sem_ar_r, sem_aa_s, sem_aa_r,
    sem_y_s, sem_y_r, sem_g_s, sem_g_r, sem_rs, sem_rr, sem_st,
):
    s = lax.axis_index("section")
    d = lax.axis_index("dp")
    n_dp = lax.axis_size("dp")
    per = n_dp // 2
    grp = lax.div(d, per)

    def differ(a, b):
        return a + b - 2 * a * b

    def mirrored(chip):
        return (3 - lax.div(chip, 4)) * 4 + lax.rem(chip, 4)

    half = differ(s, grp)
    me = jnp.where(s == 0, d, mirrored(d))
    first = (me == 0).astype(F32)
    at_z = lax.div(d, 4)
    outer = (at_z == 0) | (at_z == 3)

    def member(group, k):
        core = differ(lax.div(k, per), group)
        return (core, jnp.where(core == 0, k, mirrored(k)))

    def peer(i):
        flips = MEMBERS - 1 - i
        chip = lax.rem(d, per)
        other = grp * per
        for bit in (1, 2, 4):
            other = other + bit * differ(lax.rem(lax.div(chip, bit), 2), lax.rem(lax.div(flips, 2 * bit), 2))
        core = differ(s, lax.rem(flips, 2))
        return jnp.where(core == 0, other, mirrored(other)), (core, other)

    barrier = pltpu.get_barrier_semaphore()
    total = 2 * n_dp
    flat = s * n_dp + d

    def greet(i, c):
        other = lax.rem(flat + 1 + i, total)
        pl.semaphore_signal(
            barrier, inc=1, device_id=(lax.div(other, n_dp), lax.rem(other, n_dp)), device_id_type=MESH
        )
        return c

    lax.fori_loop(0, total - 1, greet, 0)

    own = pl.ds(2 * s, 2)
    places = [
        (red, w_r.at[own]),
        (gains, raw_g.at[s]),
        (biases, raw_b.at[s]),
        (ll, w_c.at[own, :, :, 0:CL]),
        (lg, w_c.at[own, :, :, CL:]),
        (gl, w_gl.at[own]),
        (mix, w_m.at[own]),
        (exp, w_e.at[own]),
    ]
    local_w = [pltpu.make_async_copy(a, b, sem_w.at[0, i]) for i, (a, b) in enumerate(places)]
    for c in local_w:
        c.start()

    pl.semaphore_wait(barrier, total - 1)

    across = (s, mirrored(d))
    stays = s == 0

    def across_copy(source, target, sems):
        return pltpu.make_async_remote_copy(
            source, target, sems.at[0], sems.at[1], device_id=across, device_id_type=MESH
        )

    def when_far(do):
        pl.when(jnp.logical_not(stays))(do)

    input_near = lambda: pltpu.make_async_copy(inputs.at[half], acts.at[0], sem_in.at[0, 0])

    def input_far(part):
        lanes = pl.ds(CL, CG) if part == 0 else pl.ds(0, CL)
        return across_copy(inputs.at[half, :, :, lanes], acts.at[0, :, :, lanes], sem_in.at[part])

    cot_near = lambda: pltpu.make_async_copy(cot.at[half], gblk.at[1], sem_cot.at[0, 0])

    def cot_far(row):
        return across_copy(cot.at[half, row], gblk.at[1, row], sem_cot.at[row])

    def push_rows(parity, window, do):
        if window % 2:
            row = 4 * parity + window - 1

            @pl.when(jnp.logical_not(outer))
            def _():
                do(row)
                do(row + 1)
        else:
            index = 3 * parity + window // 2
            row = jnp.where(index < 4, index, 2 * index - 4)

            @pl.when(outer)
            def _():
                do(row)
                pl.when(index >= 4)(lambda: do(row + 1))

    pl.when(stays)(lambda: input_near().start())
    when_far(lambda: input_far(0).start())
    when_far(lambda: input_far(1).start())
    partner = (1 - s, d)
    remote_w = [
        pltpu.make_async_remote_copy(
            a, b, sem_w.at[1, i], sem_w.at[2, i], device_id=partner, device_id_type=MESH
        )
        for i, (a, b) in enumerate(places)
    ]
    for c in remote_w:
        c.start()

    height = shapes[grp, 0]
    width = shapes[grp, 1]
    col = lax.broadcasted_iota(jnp.int32, (128, 128), 0)
    for q in range(PAIRS):
        for h in range(2):
            row_ok = (ROWS * me + 2 * q + h < height).astype(F32)
            pmask[q, h * 128 : (h + 1) * 128, :] = (col < width).astype(F32) * row_ok
    for f in range(4):
        f_ok = (4 * me + f <= lax.div(width, 2)).astype(F32)
        qmask[f * 128 : (f + 1) * 128, :] = (col < height).astype(F32) * f_ok
    qmask[512:640, :] = (col < height).astype(F32) * (64 <= lax.div(width, 2)).astype(F32) * first

    def inverse(count, less=0):
        return 1.0 / jnp.full((1, 128), (count - less).astype(F32))

    inv_n = inverse(height * width)
    inv_ns = inverse(height * (lax.div(width, 2) + 1))

    row_a = lax.broadcasted_iota(jnp.int32, (128, 512), 0)
    col_a = lax.broadcasted_iota(jnp.int32, (128, 512), 1)
    r_of = (col_a >> 5) * 8 + ((col_a & 31) >> 3) * 2 + (col_a & 1)
    sel_r = (row_a == r_of).astype(F32).astype(BF16)
    f_of = (col_a >> 1) & 3
    row_b = lax.broadcasted_iota(jnp.int32, (512, 128), 0)
    col_b = lax.broadcasted_iota(jnp.int32, (512, 128), 1)
    r_ob = (row_b >> 5) * 8 + ((row_b & 31) >> 3) * 2 + (row_b & 1)
    sel_rt = (col_b == r_ob).astype(F32).astype(BF16)
    f_ob = (row_b >> 1) & 3
    position = lax.broadcasted_iota(jnp.int32, (128, 128), 0)
    other_axis = lax.broadcasted_iota(jnp.int32, (128, 128), 1)

    def wave(index, side, limit, turn):
        side_real = jnp.full((128, 128), side.astype(F32))
        product = (index * other_axis).astype(F32)
        phase = product - side_real * jnp.floor((product + 0.5) / side_real)
        value = jnp.cos(phase * (2.0 * jnp.pi / side_real) + turn) * lax.rsqrt(side_real)
        return jnp.where((index < limit) & (other_axis < side), value, 0.0)

    half_turn = 0.5 * jnp.pi
    for part in range(2):
        base = wave(position, height, height, -half_turn * part).astype(BF16)
        spread = dot(base, sel_r)
        spread_t = dot(sel_rt, base)
        for f in range(4):
            hf[f, part * 128 : (part + 1) * 128, :] = jnp.where(f_of == f, spread, 0.0).astype(BF16)
            at_col = part * 512 + f * 128
            hi[:, at_col : at_col + 128] = jnp.where(f_ob == f, spread_t, 0.0).astype(BF16)
    row_c = lax.broadcasted_iota(jnp.int32, (128, 128), 0)
    sel_f = ((row_c >> 1) == lax.broadcasted_iota(jnp.int32, (128, 128), 1)).astype(F32).astype(BF16)
    half_width = lax.div(width, 2)
    lifted = jnp.where(position == 0, 64, position)
    waves = (
        wave(position, width, half_width + 1, 0.0),
        wave(lifted, width, half_width + 1, jnp.where(position == 0, 0.0, half_turn)),
    )
    weight = jnp.where((position == 0) | (position == half_width), 1.0, 2.0)
    for which, (plain, flipped_table) in enumerate(((tf, tft), (tg, tgt))):
        for part in range(2):
            spread = dot(sel_f, (waves[part] * weight if which else waves[part]).astype(BF16))
            spread_t = jnp.transpose(spread)
            for h in range(2):
                rows = slice(part * 128, (part + 1) * 128)
                cols = slice(h * 128, (h + 1) * 128)
                plain[rows, cols] = jnp.where((row_c & 1) == h, spread, 0.0).astype(BF16)
                flipped_table[cols, rows] = jnp.where(
                    (lax.broadcasted_iota(jnp.int32, (128, 128), 1) & 1) == h, spread_t, 0.0
                ).astype(BF16)
    stats[...] = jnp.zeros_like(stats)
    ssum[...] = jnp.zeros_like(ssum)
    shifted[0] = jnp.zeros((128, 1536), BF16)
    shifted[9] = jnp.zeros((128, 1536), BF16)
    gwe[...] = jnp.zeros_like(gwe)
    gwl[...] = jnp.zeros_like(gwl)

    def sums_start(slot):
        rsum[slot, me] = ssum[slot]

        def go(i, c):
            k, device = peer(i)
            pltpu.make_async_remote_copy(
                ssum.at[slot], rsum.at[slot, me], sem_ar_s.at[slot, k], sem_ar_r.at[slot, me],
                device_id=device, device_id_type=MESH,
            ).start()
            return c

        lax.fori_loop(0, MEMBERS - 1, go, 0)

    def sums_wait(slot, lanes):
        def go(i, c):
            k, device = peer(i)
            pltpu.make_async_remote_copy(
                ssum.at[slot], rsum.at[slot, k], sem_ar_s.at[slot, k], sem_ar_r.at[slot, k],
                device_id=device, device_id_type=MESH,
            ).wait()
            return c

        lax.fori_loop(0, MEMBERS - 1, go, 0)
        tot = jnp.sum(rsum[slot], axis=0)
        tiles = (lanes + 127) // 128
        one = jnp.concatenate([tot[i : i + 1] for i in range(tiles)], axis=1)[:, :lanes]
        two = jnp.concatenate([tot[4 + i : 5 + i] for i in range(tiles)], axis=1)[:, :lanes]
        return one, two

    def put_sums(slot, one, two):
        lanes = one.shape[1]
        for base_row, part in ((0, one), (4, two)):
            flat_part = jnp.sum(part, axis=0, keepdims=True)
            for i in range((lanes + 127) // 128):
                w = min(128, lanes - i * 128)
                ssum[slot, base_row + i : base_row + i + 1, 0:w] = flat_part[:, i * 128 : i * 128 + w]

    def swap_start(slot):
        recv[slot, me] = send[slot, me]

        def go(i, c):
            k, device = peer(i)
            pltpu.make_async_remote_copy(
                send.at[slot, k], recv.at[slot, me], sem_aa_s.at[slot, k], sem_aa_r.at[slot, me],
                device_id=device, device_id_type=MESH,
            ).start()
            return c

        lax.fori_loop(0, MEMBERS - 1, go, 0)

    def swap_wait(slot):
        def go(i, c):
            k, device = peer(i)
            pltpu.make_async_remote_copy(
                send.at[slot, k], recv.at[slot, k], sem_aa_s.at[slot, k], sem_aa_r.at[slot, k],
                device_id=device, device_id_type=MESH,
            ).wait()
            return c

        lax.fori_loop(0, MEMBERS - 1, go, 0)

    def halo_copies():
        up = lambda: pltpu.make_async_remote_copy(
            shifted.at[1, :, 512:1024], halo.at[1], sem_halo_s.at[0], sem_halo_r.at[1],
            device_id=member(grp, lax.rem(me + MEMBERS - 1, MEMBERS)), device_id_type=MESH,
        )
        down = lambda: pltpu.make_async_remote_copy(
            shifted.at[8, :, 512:1024], halo.at[0], sem_halo_s.at[1], sem_halo_r.at[0],
            device_id=member(grp, lax.rem(me + 1, MEMBERS)), device_id_type=MESH,
        )
        return up, down

    has_up = me > 0
    has_down = me < MEMBERS - 1

    def halo_start():
        up, down = halo_copies()

        @pl.when(has_up)
        def _():
            up().start()

        @pl.when(has_down)
        def _():
            down().start()

    def put_sides(index, x, flip):
        at_col = lax.broadcasted_iota(jnp.int32, (128, 512), 0)
        before = jnp.where(at_col == 0, 0.0, pltpu.roll(x, 1, 0)).astype(BF16)
        after = jnp.where(at_col == 127, 0.0, pltpu.roll(x, 127, 0)).astype(BF16)
        shifted[index, :, 0:512] = after if flip else before
        shifted[index, :, 1024:1536] = before if flip else after

    def put_shifted(index, row, flip):
        shifted[index, :, 512:1024] = row
        put_sides(index, row.astype(F32), flip)

    def halo_wait(flip):
        up, down = halo_copies()

        @pl.when(has_up)
        def _():
            up().wait_send()
            down().wait_recv()
            put_shifted(0, halo[0], flip)

        @pl.when(has_down)
        def _():
            down().wait_send()
            up().wait_recv()
            put_shifted(9, halo[1], flip)

    lane = lax.broadcasted_iota(jnp.int32, (128, FULL), 1)
    low = lane < HALF

    def width_out(slot, h, table, get):
        parts = []
        for q in (2 * h, 2 * h + 1):
            x = dot(table[...], get(q))
            both = jnp.concatenate([x[:128], x[128:]], axis=1)
            parts.append(both.reshape(MEMBERS, 8, FULL))
        send[slot, :, pl.ds(pl.multiple_of(16 * h, 16), 16), :] = jnp.concatenate(parts, axis=1).astype(BF16)

    def width_back(slot, h, table):
        block = recv[slot, :, pl.ds(pl.multiple_of(16 * h, 16), 16), :].astype(F32)
        results = []
        for o in range(2):
            z = block[:, 8 * o : 8 * o + 8, :].reshape(128, FULL)
            zi = pltpu.roll(z, HALF, 1)
            stacked = jnp.concatenate([z[:, :HALF], zi[:, :HALF]], axis=0).astype(BF16)
            results.append(dot(table[...], stacked))
        return results

    def rows_forward_into(slot, put):
        x = recv[slot].reshape(512, FULL)
        for f in range(4):
            both = dot(hf[f], x)
            a, b = both[:128], both[128:]
            turned = pltpu.roll(b, HALF, 1)
            if f == 0:
                rest = 1.0 - first
                put(0, jnp.where(low, a + rest * turned, rest * a - turned))
                put(4, jnp.where(low, pltpu.roll(a, HALF, 1), -b) * first)
            else:
                put(f, jnp.where(low, a + turned, a - turned))

    def rows_inverse_from(slot, get):
        last = get(4)
        for f in range(4):
            v = get(f)
            turned = pltpu.roll(v, HALF, 1)
            if f == 0:
                rest = 1.0 - first
                a = jnp.where(low, v, rest * v + first * pltpu.roll(last, HALF, 1))
                b = jnp.where(low, -turned, rest * turned - first * last)
            else:
                a = v
                b = jnp.where(low, -turned, turned)
            vab[f * 128 : (f + 1) * 128, :] = a.astype(BF16)
            vab[512 + f * 128 : 640 + f * 128, :] = b.astype(BF16)

        def go(c, carry):
            z = dot(hi[pl.ds(pl.multiple_of(c * 256, 256), 256), :], vab[...])
            send[slot, pl.ds(c * 8, 8)] = z.astype(BF16).reshape(8, 32, FULL)
            return carry

        lax.fori_loop(0, 2, go, 0)

    def moments(layer, which, lanes, one, two, inv_count):
        count = wide(inv_count, lanes)
        mean = one * count
        var = two * count - mean * mean
        inv = lax.rsqrt(var + EPSILON)
        stats[layer, which : which + 1, 0:lanes] = mean
        stats[layer, 3 + which : 4 + which, 0:lanes] = inv
        stats[layer, 6 + which : 7 + which, 0:lanes] = var
        scale = pars[layer, which : which + 1, 0:lanes] * inv
        shift = pars[layer, 3 + which : 4 + which, 0:lanes] - mean * scale
        return scale, shift

    def affine(layer, which, lanes):
        mean = stats[layer, which : which + 1, 0:lanes]
        inv = stats[layer, 3 + which : 4 + which, 0:lanes]
        gain = pars[layer, which : which + 1, 0:lanes]
        return mean, inv, gain, pars[layer, 3 + which : 4 + which, 0:lanes]

    def keep_grad_sums(layer, which, lanes, one, two):
        stats[layer, 9 + which : 10 + which, 0:lanes] = one
        stats[layer, 12 + which : 13 + which, 0:lanes] = two

    zero_of = lambda lanes: jnp.zeros((8, lanes), F32)

    def conv_pair(layer, c):
        loc = jnp.zeros((256, 512), F32)
        glo = jnp.zeros((256, 128), F32)
        for i in range(3):
            a_loc = jnp.concatenate(
                [shifted[pl.ds(2 * c + i, 2), :, j * 512 : j * 512 + 128].reshape(256, 128) for j in range(3)], axis=1
            )
            a_glo = jnp.concatenate(
                [shifted[pl.ds(2 * c + i, 2), :, j * 512 + 128 : (j + 1) * 512].reshape(256, 384) for j in range(3)],
                axis=1,
            )
            loc = loc + dot(a_loc, w_c[layer, 3 * i : 3 * i + 3].reshape(384, 512))
            glo = glo + dot(a_glo, w_gl[layer, 3 * i : 3 * i + 3].reshape(1152, 128))
        v34[layer, c, :, 0:CL] = loc[:, :CL] + glo
        v34[layer, c, :, CL:] = loc[:, CL:]

    pl.when(stays)(lambda: input_near().wait())
    when_far(lambda: input_far(0).wait())
    pl.when(stays)(lambda: cot_near().start())

    def pixel_rows(r):
        return lax.div(r, 2), pl.ds(pl.multiple_of(lax.rem(r, 2) * 128, 128), 128)

    def mask_global(r, c):
        q, here = pixel_rows(r)
        x = acts[0, r, :, CL:].astype(F32) * wide(pmask[q, here, :], CG)
        acts[0, r, :, CL:] = x.astype(BF16)
        return c

    lax.fori_loop(0, ROWS, mask_global, 0)
    for c in local_w[:3] + remote_w[:3]:
        c.wait()
    for lay in range(LAYERS):
        for base_row, raw in ((0, raw_g), (3, raw_b)):
            row = raw[lay // 2, lay % 2 : lay % 2 + 1, :]
            pars[lay, base_row : base_row + 1, 0:CS] = row[:, :CS]
            pars[lay, base_row + 1 : base_row + 2, 0:FULL] = row[:, CS : 3 * CS]
            pars[lay, base_row + 2 : base_row + 3, :] = row[:, 3 * CS :]

    def start_row(r, c):
        q, here = pixel_rows(r)
        acts[0, r, :, 0:CL] = (acts[0, r, :, 0:CL].astype(F32) * pmask[q, here, :]).astype(BF16)
        return c

    def finish_start():
        when_far(lambda: input_far(1).wait())
        lax.fori_loop(0, ROWS, start_row, 0)
        for c in local_w[3:] + remote_w[3:]:
            c.wait()

    def out_copies(source, target, sems, block, row):
        send_sem, arrive_sem = sems
        far = lambda: pltpu.make_async_remote_copy(
            source.at[row], target.at[grp, row], send_sem.at[block, row], arrive_sem.at[grp, row],
            device_id=(block, me), device_id_type=MESH,
        )
        near = lambda: pltpu.make_async_copy(source.at[row], target.at[grp, row], send_sem.at[block, row])
        return (block == s) & (me == d), far, near

    def y_copies(block, row):
        return out_copies(acts.at[2 * block + 2], out_y, (sem_y_s, sem_y_r), block, row)

    def g_copies(block, row):
        return out_copies(gblk.at[1 - block], out_g, (sem_g_s, sem_g_r), block, row)

    def start_out(made):
        here, far, near = made
        pl.when(here)(lambda: near().start())
        pl.when(jnp.logical_not(here))(lambda: far().start())

    def wait_out(made):
        here, far, near = made
        pl.when(here)(lambda: near().wait())
        pl.when(jnp.logical_not(here))(lambda: far().wait_send())

    def forward_window(layer, window):
        parity = lax.rem(layer, 2)

        @pl.when(layer < 2)
        def _():
            push_rows(parity, window, lambda row: when_far(lambda: cot_far(row).start()))

        @pl.when(layer >= 2)
        def _():
            push_rows(parity, window, lambda row: start_out(y_copies(0, row)))

    def backward_window(step, window):
        parity = lax.rem(step, 2)

        @pl.when(step < 2)
        def _():
            push_rows(parity, window, lambda row: start_out(y_copies(1, row)))

        @pl.when(step >= 2)
        def _():
            push_rows(parity, window, lambda row: start_out(g_copies(1, row)))

    def forward(layer, carry):
        def reduce_pair(q, sums):
            a = acts[layer, pl.ds(2 * q, 2), :, CL:].reshape(256, CG)
            v = dot_nt(a, w_r[layer])
            v1[layer, q] = v
            return sums[0] + fold(v), sums[1] + fold(v * v)

        put_sums(0, *lax.fori_loop(0, PAIRS, reduce_pair, (zero_of(HALF), zero_of(HALF))))
        sums_start(0)
        pl.when(layer == 0)(finish_start)

        def lay_out(r, carry):
            put_shifted(1 + r, acts[layer, r], False)
            return carry

        lax.fori_loop(0, ROWS, lay_out, 0)
        halo_start()
        forward_window(layer, 0)

        def conv_go(c, carry):
            conv_pair(layer, c)
            return carry

        lax.fori_loop(1, 3, conv_go, 0)
        scale, shift = moments(layer, 0, HALF, *sums_wait(0, HALF), inv_n)

        def spectral_in(h, carry):
            def get(q):
                pre = v1[layer, q] * scale + shift
                x = pre * sigmoid(pre) * wide(pmask[q], HALF)
                u[q] = x
                return x.astype(BF16)

            width_out(0, h, tf, get)
            return carry

        lax.fori_loop(0, 2, spectral_in, 0)
        swap_start(0)
        halo_wait(False)
        conv_pair(layer, 0)
        forward_window(layer, 1)
        swap_wait(0)

        def put(f, y):
            spec[layer, f * 128 : (f + 1) * 128, :] = y.astype(BF16)

        rows_forward_into(0, put)

        def mix_block(f, sums):
            at_row = pl.ds(pl.multiple_of(f * 128, 128), 128)
            v = dot(spec[layer, at_row, :], w_m[layer])
            mixed[layer, at_row, :] = v
            return sums[0] + fold(v), sums[1] + fold(v * v)

        put_sums(1, *lax.fori_loop(0, 5, mix_block, (zero_of(FULL), zero_of(FULL))))
        sums_start(1)
        forward_window(layer, 2)
        scale2, shift2 = moments(layer, 1, FULL, *sums_wait(1, FULL), inv_ns)

        def get_v(f):
            rows = slice(f * 128, (f + 1) * 128)
            pre = mixed[layer, rows, :] * scale2 + shift2
            return pre * sigmoid(pre) * wide(qmask[rows, :], FULL)

        rows_inverse_from(1, get_v)
        swap_start(1)
        conv_pair(layer, 3)
        forward_window(layer, 3)
        swap_wait(1)

        def spectral_out(h, sums):
            backs = width_back(1, h, tgt)
            one, two = sums
            for o in range(2):
                q = 2 * h + o
                t = (u[q] + backs[o]).astype(BF16)
                tsum[layer, q] = t
                pm = pmask[q]
                v_loc = v34[layer, q, :, 0:CL] * pm
                v_glo = (v34[layer, q, :, CL:] + dot(t, w_e[layer])) * wide(pm, CG)
                v34[layer, q, :, 0:CL] = v_loc
                v34[layer, q, :, CL:] = v_glo
                v = jnp.concatenate([v_loc, v_glo], axis=1)
                one = one + fold(v)
                two = two + fold(v * v)
            return one, two

        put_sums(2, *lax.fori_loop(0, 2, spectral_out, (zero_of(512), zero_of(512))))
        sums_start(2)
        forward_window(layer, 4)
        scale3, shift3 = moments(layer, 2, 512, *sums_wait(2, 512), inv_n)
        odd = lax.rem(layer, 2)
        oddf = odd.astype(F32)

        def next_row(r, carry):
            q = lax.div(r, 2)
            here = pl.ds(pl.multiple_of(lax.rem(r, 2) * 128, 128), 128)
            pre = v34[layer, q, here, :] * scale3 + shift3
            x = pre * sigmoid(pre) * wide(pmask[q, here, :], 512)
            x = x + oddf * acts[layer - odd, r].astype(F32)
            acts[layer + 1, r] = x.astype(BF16)
            return carry

        lax.fori_loop(0, ROWS, next_row, 0)

        return carry

    lax.fori_loop(0, LAYERS, forward, 0)

    pl.when(stays)(lambda: cot_near().wait())

    def cot_wait(row, c):
        when_far(lambda: cot_far(row).wait())
        return c

    lax.fori_loop(0, ROWS, cot_wait, 0)

    def cot_row(r, c):
        q = lax.div(r, 2)
        here = pl.ds(pl.multiple_of(lax.rem(r, 2) * 128, 128), 128)
        x = gblk[1, r].astype(F32) * wide(pmask[q, here, :], 512)
        gblk[1, r] = x.astype(BF16)
        g[q, here, :] = x
        return c

    lax.fori_loop(0, ROWS, cot_row, 0)

    x_bit = lax.rem(d, 2)
    y_bit = lax.rem(lax.div(d, 2), 2)
    at_x = jnp.where(s == 0, x_bit, y_bit)
    at_y = jnp.where(s == 0, y_bit, x_bit)
    step_x = jnp.where(s == 0, 1, 2)
    step_y = 3 - step_x
    in_core = s * 16
    in_x = in_core + at_x * 8
    in_y = in_x + at_y * 4
    near_x = (s, d + step_x * (1 - 2 * at_x))
    near_y = (s, d + step_y * (1 - 2 * at_y))

    def sum_part(p, layer):
        gw, rb, fin, out, rows = ((gwe, rbe, fine, out_we, EARLY), (gwl, rbl, finl, out_wl, LATE))[p]
        block = lax.div(layer, 2)
        odd = lax.rem(layer, 2)
        slot = jnp.where(block == s, 2, 0) + odd

        def remote(stage, source, target, other, n=0):
            return pltpu.make_async_remote_copy(
                source, target, sem_rs.at[p, odd, stage, n], sem_rr.at[p, odd, stage, n], device_id=other, device_id_type=MESH
            )

        def rows_of(first_piece, pieces):
            return pl.ds(pl.multiple_of(first_piece * rows, rows), pieces * rows)

        one = lambda: remote(0, gw.at[rows_of((1 - s) * 16, 16)], rb.at[rows_of(0, 16)], partner)
        far_x = in_core + (1 - at_x) * 8

        def two(n):
            first_four = (1 - at_y) * 4 if n == 0 else at_y * 4
            return remote(1, gw.at[rows_of(far_x + first_four, 4)], rb.at[rows_of(16 + first_four, 4)], near_x, n)

        three = lambda: remote(2, gw.at[rows_of(in_x + (1 - at_y) * 4, 4)], rb.at[rows_of(24, 4)], near_y)

        def add(first_piece, from_piece, pieces):
            def go(i, carry):
                here = rows_of(first_piece + i, 1)
                there = rows_of(from_piece + i, 1)
                gw[here, :] = (gw[here, :].astype(F32) + rb[there, :].astype(F32)).astype(BF16)
                return carry

            lax.fori_loop(0, pieces, go, 0)

        def along_z(i):
            other = lax.rem(at_z + 1 + i, 4)
            return other, (s, d + 4 * (other - at_z))

        def four(i, arriving):
            other, device = along_z(i)
            return pltpu.make_async_remote_copy(
                gw.at[rows_of(in_y + other, 1)],
                rb.at[rows_of(28 + (other if arriving else at_z), 1)],
                sem_rs.at[p, odd, 3, i], sem_rr.at[p, odd, 3, other if arriving else at_z],
                device_id=device, device_id_type=MESH,
            )

        def five(i, arriving):
            other, device = along_z(i)
            return pltpu.make_async_remote_copy(
                fin, out.at[slot, rows_of(in_y + (other if arriving else at_z), 1)],
                sem_rs.at[p, odd, 4, i], sem_rr.at[p, odd, 4, other if arriving else at_z],
                device_id=device, device_id_type=MESH,
            )

        five_own = lambda: pltpu.make_async_copy(fin, out.at[slot, rows_of(in_y + at_z, 1)], sem_rs.at[p, odd, 4, 3])

        def spread_copy(stage, first_piece, other, n=0):
            here = out.at[slot, rows_of(first_piece, 4)]
            return remote(stage, here, here, other, n)

        six = lambda: spread_copy(5, in_y, near_y)
        seven = lambda n: spread_copy(6, in_y if n == 0 else in_x + (1 - at_y) * 4, near_x, n)
        eight = lambda: remote(
            7, out.at[odd, rows_of(in_core, 16)],
            out.at[2 + odd, rows_of(in_core, 16)], partner,
        )
        starts = s != block

        def begin_one():
            one().start()

        def begin_two():
            one().wait()
            add(in_core, 0, 16)
            two(0).start()

        def begin_three():
            two(0).wait()
            add(in_x + (1 - at_y) * 4, 16 + (1 - at_y) * 4, 4)
            two(1).start()
            three().start()

        def begin_four():
            two(1).wait()
            three().wait()
            add(in_y, 16 + at_y * 4, 4)
            add(in_y, 24, 4)
            for i in range(3):
                four(i, False).start()

        def begin_five():
            total_now = gw[rows_of(in_y + at_z, 1), :].astype(F32)
            for i in range(3):
                four(i, False).wait_send()
                four(i, True).wait_recv()
                total_now = total_now + rb[rows_of(28 + lax.rem(at_z + 1 + i, 4), 1), :].astype(F32)
            fin[...] = total_now.astype(BF16)
            five_own().start()
            for i in range(3):
                five(i, False).start()

        def begin_six():
            five_own().wait()
            for i in range(3):
                five(i, False).wait_send()
                five(i, True).wait_recv()
            six().start()
            seven(0).start()

        def begin_seven():
            six().wait()
            seven(0).wait()
            seven(1).start()

        def begin_eight():
            seven(1).wait()
            pl.when(starts)(lambda: eight().start())

        def end():
            pl.when(starts)(lambda: eight().wait_send())
            pl.when(jnp.logical_not(starts))(lambda: eight().wait_recv())

        return (
            begin_one, begin_two, begin_three, begin_four, begin_five,
            begin_six, begin_seven, begin_eight, end,
        )

    def stage(p, layer, which):
        pl.when(layer < LAYERS)(lambda: sum_part(p, layer)[which]())

    def backward(step, carry):
        layer = LAYERS - 1 - step
        mean3, inv3, gain3, bias3 = affine(layer, 2, 512)
        scale3 = gain3 * inv3
        shift3 = bias3 - mean3 * scale3

        def slope_row(r, sums):
            q = lax.div(r, 2)
            here = pl.ds(pl.multiple_of(lax.rem(r, 2) * 128, 128), 128)
            v = v34[layer, q, here, :]
            pre = v * scale3 + shift3
            sg = sigmoid(pre)
            e = g[q, here, :] * wide(pmask[q, here, :], 512) * (sg * (1.0 + pre * (1.0 - sg)))
            g[q, here, :] = e
            return sums[0] + fold(e), sums[1] + fold(e * ((v - mean3) * inv3))

        put_sums(3, *lax.fori_loop(0, ROWS, slope_row, (zero_of(512), zero_of(512))))
        sums_start(3)
        backward_window(step, 0)

        def turn_row(r, carry):
            at[:, pl.ds(pl.multiple_of(r * 128, 128), 128)] = jnp.transpose(acts[layer, r])
            return carry

        stage(0, layer + 1, 4)
        stage(1, layer + 1, 1)
        stage(1, layer + 2, 6)
        lax.fori_loop(0, ROWS, turn_row, 0)
        one3, two3 = sums_wait(3, 512)
        keep_grad_sums(layer, 2, 512, one3, two3)
        part_a = one3 * wide(inv_n, 512)
        part_b = two3 * wide(inv_n, 512)

        def d_row(r, carry):
            q = lax.div(r, 2)
            here = pl.ds(pl.multiple_of(lax.rem(r, 2) * 128, 128), 128)
            z = (v34[layer, q, here, :] - mean3) * inv3
            dv = wide(pmask[q, here, :], 512) * scale3 * (g[q, here, :] - part_a - z * part_b)
            shifted[1 + r, :, 512:1024] = dv.astype(BF16)
            return carry

        lax.fori_loop(0, ROWS, d_row, 0)
        halo_start()

        def grad_out(h, carry):
            def get(q):
                dg = shifted[pl.ds(1 + 2 * q, 2), :, 512 + CL : 1024].reshape(256, CG)
                dt = dot_nt(dg, w_e[layer])
                u[q] = dt
                return dt.astype(BF16)

            width_out(0, h, tg, get)
            return carry

        lax.fori_loop(0, 2, grad_out, 0)
        swap_start(0)

        def lay_sides(r, carry):
            put_sides(1 + r, shifted[1 + r, :, 512:1024].astype(F32), True)
            return carry

        lax.fori_loop(0, ROWS, lay_sides, 0)
        halo_wait(True)

        def conv_back(c, carry):
            d_loc = jnp.zeros((256, 128), F32)
            d_glo = jnp.zeros((256, 384), F32)
            for i in range(3):
                for j in range(3):
                    rows = pl.ds(2 * c + 2 - i, 2)
                    dd = shifted[rows, :, j * 512 : (j + 1) * 512].reshape(256, 512)
                    d_loc = d_loc + dot_nt(dd, w_c[layer, 3 * i + j])
                    d_glo = d_glo + dot_nt(dd[:, :CL], w_gl[layer, 3 * i + j])
            g[c, :, 0:CL] = d_loc
            g[c, :, CL:] = d_glo
            return carry

        def block_rows(i, lanes):
            return jnp.concatenate(
                [
                    shifted[2 - i : 10 - i, :, j * 512 + lanes[0] : j * 512 + lanes[1]].reshape(1024, lanes[1] - lanes[0])
                    for j in range(3)
                ],
                axis=1,
            )

        def lift_grad(i):
            acc = dot(at[0:CL, :], block_rows(i, (CL, 512)))
            for j in range(3):
                for n in range(3):
                    base = AT_KG + n * 1152 + (3 * i + j) * 128
                    gwe[base : base + 128, :] = acc[:, (3 * j + n) * 128 : (3 * j + n + 1) * 128].astype(BF16)

        def local_grad(i):
            acc = dot(at[...], block_rows(i, (0, CL)))
            for j in range(3):
                tap = 3 * i + j
                block = acc[:, j * 128 : (j + 1) * 128].astype(BF16)
                gwe[AT_LL + tap * CL : AT_LL + (tap + 1) * CL, :] = block[:CL]
                gwe[AT_GL + tap * CG : AT_GL + (tap + 1) * CG, :] = block[CL:]

        conv_back(0, 0)
        stage(0, layer + 1, 5)
        stage(1, layer + 2, 7)
        stage(1, layer + 1, 2)
        backward_window(step, 1)
        for i in range(3):
            local_grad(i)
        swap_wait(0)

        def put(f, y):
            e2[f * 128 : (f + 1) * 128, :] = y

        rows_forward_into(0, put)
        mean2, inv2, gain2, bias2 = affine(layer, 1, FULL)
        scale2 = gain2 * inv2
        shift2 = bias2 - mean2 * scale2

        def slope_block(f, sums):
            rows = pl.ds(pl.multiple_of(f * 128, 128), 128)
            v = mixed[layer, rows, :]
            pre = v * scale2 + shift2
            sg = sigmoid(pre)
            e = e2[rows, :] * wide(qmask[rows, :], FULL) * (sg * (1.0 + pre * (1.0 - sg)))
            e2[rows, :] = e
            return sums[0] + fold(e), sums[1] + fold(e * ((v - mean2) * inv2))

        put_sums(1, *lax.fori_loop(0, 5, slope_block, (zero_of(FULL), zero_of(FULL))))
        sums_start(1)
        backward_window(step, 2)
        stage(0, layer + 1, 6)
        stage(1, layer + 2, 8)
        stage(1, layer + 1, 3)
        for i in range(3):
            lift_grad(i)
        acc_e = jnp.zeros((HALF, CG), F32)
        for q in range(PAIRS):
            dg = shifted[1 + 2 * q : 3 + 2 * q, :, 512 + CL : 1024].reshape(256, CG)
            acc_e = acc_e + dot_tn(tsum[layer, q], dg)
        for n in range(3):
            gwe[AT_E + n * HALF : AT_E + (n + 1) * HALF, :] = acc_e[:, n * 128 : (n + 1) * 128].astype(BF16)
        stage(0, layer, 0)
        one2, two2 = sums_wait(1, FULL)
        stage(0, layer, 1)
        keep_grad_sums(layer, 1, FULL, one2, two2)
        part_a2 = one2 * wide(inv_ns, FULL)
        part_b2 = two2 * wide(inv_ns, FULL)

        def dq_block(f, carry):
            rows = pl.ds(pl.multiple_of(f * 128, 128), 128)
            z = (mixed[layer, rows, :] - mean2) * inv2
            dv = wide(qmask[rows, :], FULL) * scale2 * (e2[rows, :] - part_a2 - z * part_b2)
            low_dv = dv.astype(BF16)
            dq[rows, :] = low_dv
            e2[rows, :] = dot_nt(low_dv, w_m[layer])
            return carry

        lax.fori_loop(0, 5, dq_block, 0)
        rows_inverse_from(1, lambda f: e2[f * 128 : (f + 1) * 128, :])
        swap_start(1)
        conv_back(1, 0)
        stage(0, layer, 2)
        stage(0, layer + 1, 7)
        stage(1, layer + 1, 4)
        backward_window(step, 3)
        conv_back(2, 0)
        swap_wait(1)

        mean1, inv1, gain1, bias1 = affine(layer, 0, HALF)
        scale1 = gain1 * inv1
        shift1 = bias1 - mean1 * scale1

        def slope_in(h, sums):
            backs = width_back(1, h, tft)
            one, two = sums
            for o in range(2):
                q = 2 * h + o
                v = v1[layer, q]
                pre = v * scale1 + shift1
                sg = sigmoid(pre)
                e = (u[q] + backs[o]) * wide(pmask[q], HALF) * (sg * (1.0 + pre * (1.0 - sg)))
                u[q] = e
                one = one + fold(e)
                two = two + fold(e * ((v - mean1) * inv1))
            return one, two

        put_sums(0, *lax.fori_loop(0, 2, slope_in, (zero_of(HALF), zero_of(HALF))))
        sums_start(0)
        backward_window(step, 4)
        stage(0, layer, 3)
        stage(0, layer + 1, 8)
        stage(1, layer + 1, 5)
        conv_back(3, 0)
        acc_m = jnp.zeros((FULL, FULL), F32)
        for f in range(5):
            rows = slice(f * 128, (f + 1) * 128)
            acc_m = acc_m + dot_tn(spec[layer, rows, :], dq[rows, :])
        for n in range(3):
            gwl[AT_M + n * FULL : AT_M + (n + 1) * FULL, :] = acc_m[:, n * 128 : (n + 1) * 128].astype(BF16)
        one1, two1 = sums_wait(0, HALF)
        keep_grad_sums(layer, 0, HALF, one1, two1)
        part_a1 = one1 * wide(inv_n, HALF)
        part_b1 = two1 * wide(inv_n, HALF)

        def ds_pair(q, carry):
            z = (v1[layer, q] - mean1) * inv1
            dv = wide(pmask[q], HALF) * scale1 * (u[q] - part_a1 - z * part_b1)
            low_dv = dv.astype(BF16)
            ds[q] = low_dv
            g[q, :, CL:] = g[q, :, CL:] + dot(low_dv, w_r[layer])
            return carry

        lax.fori_loop(0, PAIRS, ds_pair, 0)
        acc_r = jnp.zeros((HALF, CG), F32)
        for q in range(PAIRS):
            a = acts[layer, 2 * q : 2 * q + 2, :, CL:].reshape(256, CG)
            acc_r = acc_r + dot_tn(ds[q], a)
        for n in range(3):
            gwl[AT_R + n * HALF : AT_R + (n + 1) * HALF, :] = acc_r[:, n * 128 : (n + 1) * 128].astype(BF16)

        stage(1, layer, 0)

        @pl.when(lax.rem(layer, 2) == 0)
        def _():
            block = lax.div(layer, 2)

            def close_row(r, carry):
                q = lax.div(r, 2)
                here = pl.ds(pl.multiple_of(lax.rem(r, 2) * 128, 128), 128)
                x = (gblk[block, r].astype(F32) + g[q, here, :]) * wide(pmask[q, here, :], 512)
                low_x = x.astype(BF16)
                gblk[1 - block, r] = low_x
                g[q, here, :] = low_x.astype(F32)

                return carry

            lax.fori_loop(0, ROWS, close_row, 0)

        return carry

    lax.fori_loop(0, LAYERS, backward, 0)

    far = pltpu.make_async_remote_copy(
        stats.at[own], stats_far, sem_st.at[0], sem_st.at[1],
        device_id=across, device_id_type=MESH,
    )
    far.start()

    def push_last(first_row, rows):
        for row in range(first_row, first_row + rows):
            start_out(g_copies(0, row))

    stage(0, 0, 4)
    stage(1, 1, 6)
    push_last(0, 1)
    stage(1, 0, 1)
    stage(1, 0, 2)
    stage(1, 1, 7)
    stage(1, 0, 3)
    push_last(1, 2)
    stage(0, 0, 5)
    stage(1, 0, 4)
    push_last(3, 5)
    stage(1, 1, 8)
    stage(0, 0, 6)
    stage(1, 0, 5)
    stage(0, 0, 7)
    stage(1, 0, 6)
    stage(1, 0, 7)
    stage(0, 0, 8)
    stage(1, 0, 8)
    for block in range(2):
        def sent(row, carry, block=block):
            wait_out(y_copies(block, row))
            wait_out(g_copies(block, row))
            return carry

        lax.fori_loop(0, ROWS, sent, 0)
    for m in range(2):
        sender = member(m, d)
        from_self = (sender[0] == s) & (sender[1] == d)

        def arrived(row, carry, m=m):
            for source, target, sems in ((acts, out_y, (sem_y_s, sem_y_r)), (gblk, out_g, (sem_g_s, sem_g_r))):
                pltpu.make_async_remote_copy(
                    source.at[0, row], target.at[m, row], sems[0].at[0, row], sems[1].at[m, row],
                    device_id=partner, device_id_type=MESH,
                ).wait_recv()
            return carry

        @pl.when(jnp.logical_not(from_self))
        def _(arrived=arrived):
            lax.fori_loop(0, ROWS, arrived, 0)

    far.wait()
    for lay in range(2):
        mine = stats[2 * s + lay]
        other = stats_far[lay]
        zero_first = jnp.where(grp == 0, mine, other)
        one_next = jnp.where(grp == 0, other, mine)
        row = slice(lay, lay + 1)

        def joined(st, base):
            return jnp.concatenate(
                [st[base : base + 1, :HALF], st[base + 1 : base + 2, :FULL], st[base + 2 : base + 3]], axis=1
            )

        mean = run_m[row, :]
        var = run_v[row, :]
        for m, st in enumerate((zero_first, one_next)):
            pixels = shapes[m, 0] * shapes[m, 1]
            points = shapes[m, 0] * (lax.div(shapes[m, 1], 2) + 1)
            fix = [
                wide(jnp.full((1, 128), count.astype(F32)) * inverse(count, 1), lanes)
                for count, lanes in ((pixels, HALF), (points, FULL), (pixels, 512))
            ]
            mean = (1.0 - MOMENTUM) * mean + MOMENTUM * joined(st, 0)
            var = (1.0 - MOMENTUM) * var + MOMENTUM * joined(st, 6) * jnp.concatenate(fix, axis=1)
        out_m[row, :] = mean
        out_v[row, :] = var
        out_biases[row, :] = joined(zero_first, 9) + joined(one_next, 9)
        out_gains[row, :] = joined(zero_first, 12) + joined(one_next, 12)


def tiles_of(rows, array):
    return jnp.concatenate([array[:, n * rows : (n + 1) * rows].astype(F32) for n in range(3)], axis=-1)


def on_band(
    inputs,
    cotangent,
    shapes,
    local_to_local,
    global_to_local,
    local_to_global,
    spec_reduce,
    spec_mix,
    spec_expand,
    norm_gains,
    norm_biases,
    run_means,
    run_vars,
):
    anywhere = pl.BlockSpec(memory_space=pl.ANY)
    vmem = pl.BlockSpec(memory_space=pltpu.VMEM)
    dma = pltpu.SemaphoreType.DMA
    band = (ROWS, LONG, 512)
    out_y, out_g, out_we, out_wl, *out_norms = pl.pallas_call(
        network_kernel,
        out_shape=(
            jax.ShapeDtypeStruct((2,) + band, BF16),
            jax.ShapeDtypeStruct((2,) + band, BF16),
            jax.ShapeDtypeStruct((4, PIECES * EARLY, 128), BF16),
            jax.ShapeDtypeStruct((4, PIECES * LATE, 128), BF16),
            *[jax.ShapeDtypeStruct((2, 3 * CS + 512), F32)] * 4,
        ),
        in_specs=[anywhere, anywhere, pl.BlockSpec(memory_space=pltpu.SMEM)]
        + [anywhere] * 8
        + [vmem] * 2,
        out_specs=(anywhere,) * 4 + (vmem,) * 4,
        scratch_shapes=[
            pltpu.VMEM((LAYERS, 9, CL, 512), BF16),
            pltpu.VMEM((LAYERS, 9, CG, CL), BF16),
            pltpu.VMEM((LAYERS, CS, CG), BF16),
            pltpu.VMEM((LAYERS, FULL, FULL), BF16),
            pltpu.VMEM((LAYERS, CS, CG), BF16),
            pltpu.VMEM((2, 2, 3 * CS + 512), F32),
            pltpu.VMEM((2, 2, 3 * CS + 512), F32),
            pltpu.VMEM((LAYERS, 8, 512), F32),
            pltpu.VMEM((LAYERS + 1,) + band, BF16),
            pltpu.VMEM((ROWS + 2, LONG, 1536), BF16),
            pltpu.VMEM((2, LONG, 512), BF16),
            pltpu.VMEM((LAYERS, PAIRS, 256, CS), F32),
            pltpu.VMEM((PAIRS, 256, CS), F32),
            pltpu.VMEM((LAYERS, SLOTS, FULL), BF16),
            pltpu.VMEM((LAYERS, SLOTS, FULL), F32),
            pltpu.VMEM((LAYERS, PAIRS, 256, CS), BF16),
            pltpu.VMEM((LAYERS, PAIRS, 256, 512), F32),
            pltpu.VMEM((PAIRS, 256, 128), F32),
            pltpu.VMEM((SLOTS, 128), F32),
            pltpu.VMEM((256, 256), BF16),
            pltpu.VMEM((256, 256), BF16),
            pltpu.VMEM((256, 256), BF16),
            pltpu.VMEM((256, 256), BF16),
            pltpu.VMEM((4, 256, 512), BF16),
            pltpu.VMEM((512, 1024), BF16),
            pltpu.VMEM((1024, FULL), BF16),
            pltpu.VMEM((SLOTS, FULL), F32),
            pltpu.VMEM((SLOTS, FULL), BF16),
            pltpu.VMEM((PAIRS, 256, CS), BF16),
            pltpu.VMEM((PAIRS, 256, 512), F32),
            pltpu.VMEM((2,) + band, BF16),
            pltpu.VMEM((512, ROWS * LONG), BF16),
            pltpu.VMEM((PIECES * EARLY, 128), BF16),
            pltpu.VMEM((PIECES * LATE, 128), BF16),
            pltpu.VMEM((PIECES * EARLY, 128), BF16),
            pltpu.VMEM((PIECES * LATE, 128), BF16),
            pltpu.VMEM((EARLY, 128), BF16),
            pltpu.VMEM((LATE, 128), BF16),
            pltpu.VMEM((4, 8, 128), F32),
            pltpu.VMEM((4, MEMBERS, 8, 128), F32),
            pltpu.VMEM((2, MEMBERS, 32, FULL), BF16),
            pltpu.VMEM((2, MEMBERS, 32, FULL), BF16),
            pltpu.VMEM((LAYERS, 16, 512), F32),
            pltpu.VMEM((2, 16, 512), F32),
            dma((3, 8)),
            dma((2, 2)),
            dma((ROWS, 2)),
            dma((2,)),
            dma((2,)),
            dma((4, MEMBERS)),
            dma((4, MEMBERS)),
            dma((2, MEMBERS)),
            dma((2, MEMBERS)),
            dma((2, ROWS)),
            dma((2, ROWS)),
            dma((2, ROWS)),
            dma((2, ROWS)),
            dma((2, 2, 8, 4)),
            dma((2, 2, 8, 4)),
            dma((2,)),
        ],
        compiler_params=pltpu.CompilerParams(
            collective_id=0, has_side_effects=True, vmem_limit_bytes=63 << 20
        ),
        name="network",
    )(
        inputs[:, 0],
        cotangent[:, 0],
        shapes,
        local_to_local[0],
        global_to_local[0],
        local_to_global[0],
        jnp.swapaxes(spec_reduce[0], 1, 2),
        spec_mix[0],
        spec_expand[0],
        norm_gains[0],
        norm_biases[0],
        run_means[0],
        run_vars[0],
    )
    grad_ll = out_we[2:, AT_LL:AT_GL].astype(F32).reshape(2, 9, CL, CL)
    grad_gl = out_we[2:, AT_GL:AT_KG].astype(F32).reshape(2, 9, CG, CL)
    grad_lift = tiles_of(9 * CL, out_we[2:, AT_KG:AT_E]).reshape(2, 9, CL, CG)
    grad_expand = tiles_of(CS, out_we[2:, AT_E:])
    grad_mix = tiles_of(FULL, out_wl[2:, AT_M:])
    grad_reduce = jnp.swapaxes(tiles_of(CS, out_wl[2:, AT_R:]), 1, 2)
    out_gains, out_biases, out_means, out_vars = out_norms
    return (
        out_y[None, :, None],
        out_g.astype(F32)[None, :, None],
        grad_ll[None],
        grad_gl[None],
        grad_lift[None],
        grad_reduce[None],
        grad_mix[None],
        grad_expand[None],
        out_gains[None],
        out_biases[None],
        out_means[None],
        out_vars[None],
    )


def solution(mesh):
    in_specs = (
        P(None, None, "dp", None, None),
        P(None, None, "dp", None, None),
        P(),
        P("section", None, None, None, None),
        P("section", None, None, None, None),
        P("section", None, None, None, None),
        P("section", None, None, None),
        P("section", None, None, None),
        P("section", None, None, None),
        P("section", None, None),
        P("section", None, None),
        P("section", None, None),
        P("section", None, None),
    )
    out_specs = (
        P("section", None, None, "dp", None, None),
        P("section", None, None, "dp", None, None),
        P("section", None, None, None, None),
        P("section", None, None, None, None),
        P("section", None, None, None, None),
        P("section", None, None, None),
        P("section", None, None, None),
        P("section", None, None, None),
        P("section", None, None),
        P("section", None, None),
        P("section", None, None),
        P("section", None, None),
    )
    dp_size = mesh.shape["dp"]
    banded = dp_size == MEMBERS and LONG == dp_size * ROWS
    return jax.shard_map(
        on_band if banded else on_device, mesh=mesh, in_specs=in_specs, out_specs=out_specs, check_vma=False
    )
```

profile of v0, /device:TPU:0, one launch (start us, length us, event | category | flops | bytes accessed | tf_op | source)
XLA Modules:
  0.0 442.1 jit_solution(1541325432858665467)
XLA Ops:
  0.6 420.9 %network.1 = (bf16[2,8,128,512]{3,2,1,0:T(8,128)(2,1)}, bf16[2,8,128,512]{3,2,1,0:T(8,128)(2,1)}, bf16[4,8704,128]{2,1,0:T(8,128)(2,1)}, bf16[4,2048,128]{2,1,0:...) custom-call(bf16[2,8,128,512]{3,2,1,0:T(8,128)(2,1)} %bitcast.51, ...), custom_call_target="tpu_custom_call" | custom-call | tf_op jit(solution)/shard_map/network/pallas_call | solution.py:1678
  421.5 1.2 fusion.2
  422.7 1.2 fusion.4
  423.9 0.9 fusion.1
  424.7 0.9 convert_bitcast_fusion
  425.6 1.1 fusion
  426.7 1.6 slice.59
  428.3 1.8 fusion.3
  430.1 0.2 pad_maximum_fusion
  430.3 1.1 convert.14
  431.4 2.2 convert.15
  433.6 0.0 copy-start
  433.6 2.2 convert.16
  435.8 0.0 copy-done
  435.8 0.0 copy-start.1
  435.8 2.6 bitcast_convert_fusion
  438.4 0.0 copy-done.1
  438.4 0.0 copy-start.5
  438.4 0.0 copy-start.4
  438.4 0.0 copy-start.3
  438.4 0.0 copy-start.2
  438.4 1.3 copy.32
  439.7 0.0 copy-done.5
  439.7 0.6 copy.33
  440.3 0.0 copy-done.4
  440.3 0.6 copy.34
  440.9 0.0 copy-done.3
  440.9 0.6 copy.35
  441.5 0.0 copy-done.2
  441.5 0.6 copy.36
Async XLA Ops:
  433.6 2.2 copy-start
  435.8 2.6 copy-start.1
  438.4 1.3 copy-start.5
  438.4 1.9 copy-start.4
  438.4 2.5 copy-start.3
  438.4 3.1 copy-start.2
where the time goes:
time: 442 us
  Pallas kernels  421 us (95%)
  other arithmetic  11.1 us (3%)
  local copies, waits for them, and re-layouts  9.45 us (2%)
    pallas_call x1, Pallas kernels, on_band(): pl.pallas_call(network_kernel, out_shape=(jax.ShapeDtypeStruct((2,) + ban...  421 us

commit v1 on v0

--- a/solution.py
+++ b/solution.py
@@ -1108,10 +1108,10 @@
 
         rows_forward_into(0, put)
 
+        mixed[layer] = dot(spec[layer], w_m[layer])
+
         def mix_block(f, sums):
-            at_row = pl.ds(pl.multiple_of(f * 128, 128), 128)
-            v = dot(spec[layer, at_row, :], w_m[layer])
-            mixed[layer, at_row, :] = v
+            v = mixed[layer, pl.ds(pl.multiple_of(f * 128, 128), 128), :]
             return sums[0] + fold(v), sums[1] + fold(v * v)
 
         put_sums(1, *lax.fori_loop(0, 5, mix_block, (zero_of(FULL), zero_of(FULL))))
@@ -1273,17 +1273,16 @@
             one().wait()
             add(in_core, 0, 16)
             two(0).start()
+            two(1).start()
 
         def begin_three():
             two(0).wait()
-            add(in_x + (1 - at_y) * 4, 16 + (1 - at_y) * 4, 4)
-            two(1).start()
+            two(1).wait()
+            add(in_x, 16, 8)
             three().start()
 
         def begin_four():
-            two(1).wait()
             three().wait()
-            add(in_y, 16 + at_y * 4, 4)
             add(in_y, 24, 4)
             for i in range(3):
                 four(i, False).start()
@@ -1299,20 +1298,23 @@
             for i in range(3):
                 five(i, False).start()
 
-        def begin_six():
+        def begin_six(quick):
             five_own().wait()
             for i in range(3):
                 five(i, False).wait_send()
                 five(i, True).wait_recv()
             six().start()
-            seven(0).start()
-
-        def begin_seven():
+            if quick:
+                seven(0).start()
+
+        def begin_seven(quick):
             six().wait()
+            if not quick:
+                seven(0).start()
+            seven(1).start()
+
+        def begin_eight():
             seven(0).wait()
-            seven(1).start()
-
-        def begin_eight():
             seven(1).wait()
             pl.when(starts)(lambda: eight().start())
 
@@ -1322,8 +1324,11 @@
 
         return (
             begin_one, begin_two, begin_three, begin_four, begin_five,
-            begin_six, begin_seven, begin_eight, end,
+            lambda: begin_six(False), lambda: begin_seven(False), begin_eight, end,
+            lambda: begin_six(True), lambda: begin_seven(True),
         )
+
+    QUICK_SIX, QUICK_SEVEN = 9, 10
 
     def stage(p, layer, which):
         pl.when(layer < LAYERS)(lambda: sum_part(p, layer)[which]())
@@ -1352,9 +1357,10 @@
             at[:, pl.ds(pl.multiple_of(r * 128, 128), 128)] = jnp.transpose(acts[layer, r])
             return carry
 
-        stage(0, layer + 1, 4)
+        stage(0, layer + 1, 3)
+        stage(0, layer + 2, 6)
         stage(1, layer + 1, 1)
-        stage(1, layer + 2, 6)
+        stage(1, layer + 2, QUICK_SEVEN)
         lax.fori_loop(0, ROWS, turn_row, 0)
         one3, two3 = sums_wait(3, 512)
         keep_grad_sums(layer, 2, 512, one3, two3)
@@ -1429,38 +1435,12 @@
                 gwe[AT_LL + tap * CL : AT_LL + (tap + 1) * CL, :] = block[:CL]
                 gwe[AT_GL + tap * CG : AT_GL + (tap + 1) * CG, :] = block[CL:]
 
-        conv_back(0, 0)
-        stage(0, layer + 1, 5)
         stage(1, layer + 2, 7)
         stage(1, layer + 1, 2)
         backward_window(step, 1)
+        stage(0, layer + 1, 4)
         for i in range(3):
             local_grad(i)
-        swap_wait(0)
-
-        def put(f, y):
-            e2[f * 128 : (f + 1) * 128, :] = y
-
-        rows_forward_into(0, put)
-        mean2, inv2, gain2, bias2 = affine(layer, 1, FULL)
-        scale2 = gain2 * inv2
-        shift2 = bias2 - mean2 * scale2
-
-        def slope_block(f, sums):
-            rows = pl.ds(pl.multiple_of(f * 128, 128), 128)
-            v = mixed[layer, rows, :]
-            pre = v * scale2 + shift2
-            sg = sigmoid(pre)
-            e = e2[rows, :] * wide(qmask[rows, :], FULL) * (sg * (1.0 + pre * (1.0 - sg)))
-            e2[rows, :] = e
-            return sums[0] + fold(e), sums[1] + fold(e * ((v - mean2) * inv2))
-
-        put_sums(1, *lax.fori_loop(0, 5, slope_block, (zero_of(FULL), zero_of(FULL))))
-        sums_start(1)
-        backward_window(step, 2)
-        stage(0, layer + 1, 6)
-        stage(1, layer + 2, 8)
-        stage(1, layer + 1, 3)
         for i in range(3):
             lift_grad(i)
         acc_e = jnp.zeros((HALF, CG), F32)
@@ -1470,8 +1450,35 @@
         for n in range(3):
             gwe[AT_E + n * HALF : AT_E + (n + 1) * HALF, :] = acc_e[:, n * 128 : (n + 1) * 128].astype(BF16)
         stage(0, layer, 0)
+        swap_wait(0)
+
+        def put(f, y):
+            e2[f * 128 : (f + 1) * 128, :] = y
+
+        rows_forward_into(0, put)
+        mean2, inv2, gain2, bias2 = affine(layer, 1, FULL)
+        scale2 = gain2 * inv2
+        shift2 = bias2 - mean2 * scale2
+
+        def slope_block(f, sums):
+            rows = pl.ds(pl.multiple_of(f * 128, 128), 128)
+            v = mixed[layer, rows, :]
+            pre = v * scale2 + shift2
+            sg = sigmoid(pre)
+            e = e2[rows, :] * wide(qmask[rows, :], FULL) * (sg * (1.0 + pre * (1.0 - sg)))
+            e2[rows, :] = e
+            return sums[0] + fold(e), sums[1] + fold(e * ((v - mean2) * inv2))
+
+        put_sums(1, *lax.fori_loop(0, 5, slope_block, (zero_of(FULL), zero_of(FULL))))
+        sums_start(1)
+        backward_window(step, 2)
+        stage(1, layer + 2, 8)
+        stage(1, layer + 1, 3)
+        conv_back(0, 0)
+        stage(0, layer, 1)
+        stage(0, layer + 2, 7)
+        conv_back(1, 0)
         one2, two2 = sums_wait(1, FULL)
-        stage(0, layer, 1)
         keep_grad_sums(layer, 1, FULL, one2, two2)
         part_a2 = one2 * wide(inv_ns, FULL)
         part_b2 = two2 * wide(inv_ns, FULL)
@@ -1480,20 +1487,18 @@
             rows = pl.ds(pl.multiple_of(f * 128, 128), 128)
             z = (mixed[layer, rows, :] - mean2) * inv2
             dv = wide(qmask[rows, :], FULL) * scale2 * (e2[rows, :] - part_a2 - z * part_b2)
-            low_dv = dv.astype(BF16)
-            dq[rows, :] = low_dv
-            e2[rows, :] = dot_nt(low_dv, w_m[layer])
+            dq[rows, :] = dv.astype(BF16)
             return carry
 
         lax.fori_loop(0, 5, dq_block, 0)
+        e2[...] = dot_nt(dq[...], w_m[layer])
         rows_inverse_from(1, lambda f: e2[f * 128 : (f + 1) * 128, :])
         swap_start(1)
-        conv_back(1, 0)
-        stage(0, layer, 2)
-        stage(0, layer + 1, 7)
+        conv_back(2, 0)
         stage(1, layer + 1, 4)
         backward_window(step, 3)
-        conv_back(2, 0)
+        conv_back(3, 0)
+        pl.when(layer == 0)(lambda: stage(0, 0, 2))
         swap_wait(1)
 
         mean1, inv1, gain1, bias1 = affine(layer, 0, HALF)
@@ -1517,10 +1522,11 @@
         put_sums(0, *lax.fori_loop(0, 2, slope_in, (zero_of(HALF), zero_of(HALF))))
         sums_start(0)
         backward_window(step, 4)
-        stage(0, layer, 3)
-        stage(0, layer + 1, 8)
-        stage(1, layer + 1, 5)
-        conv_back(3, 0)
+        pl.when(layer > 0)(lambda: stage(0, layer, 2))
+        pl.when(layer == 0)(lambda: stage(0, 0, 3))
+        stage(0, layer + 1, 5)
+        stage(0, layer + 2, 8)
+        stage(1, layer + 1, QUICK_SIX)
         acc_m = jnp.zeros((FULL, FULL), F32)
         for f in range(5):
             rows = slice(f * 128, (f + 1) * 128)
@@ -1548,6 +1554,7 @@
         for n in range(3):
             gwl[AT_R + n * HALF : AT_R + (n + 1) * HALF, :] = acc_r[:, n * 128 : (n + 1) * 128].astype(BF16)
 
+
         stage(1, layer, 0)
 
         @pl.when(lax.rem(layer, 2) == 0)
@@ -1581,21 +1588,24 @@
             start_out(g_copies(0, row))
 
     stage(0, 0, 4)
-    stage(1, 1, 6)
+    stage(1, 1, QUICK_SEVEN)
     push_last(0, 1)
     stage(1, 0, 1)
     stage(1, 0, 2)
     stage(1, 1, 7)
+    stage(0, 1, 6)
     stage(1, 0, 3)
     push_last(1, 2)
-    stage(0, 0, 5)
+    stage(0, 0, QUICK_SIX)
     stage(1, 0, 4)
     push_last(3, 5)
     stage(1, 1, 8)
-    stage(0, 0, 6)
-    stage(1, 0, 5)
+    stage(0, 1, 7)
+    stage(1, 0, QUICK_SIX)
+    stage(0, 0, QUICK_SEVEN)
+    stage(1, 0, QUICK_SEVEN)
+    stage(0, 1, 8)
     stage(0, 0, 7)
-    stage(1, 0, 6)
     stage(1, 0, 7)
     stage(0, 0, 8)
     stage(1, 0, 8)

time: 442 us -> 432 us (0.977)
  Pallas kernels: 421 us -> 409 us
    pallas_call x1, Pallas kernels: 421 us -> 409 us  [on_band(): pl.pallas_call(network_kernel, out_shape=(jax.ShapeDtypeStruct((2,) + ban...]
where the time goes in v1:
time: 432 us; the launch traced here: 430 us
  Pallas kernels  409 us (95%)
  other arithmetic  11.1 us (3%)
  local copies, waits for them, and re-layouts  9.45 us (2%)
    pallas_call x1, Pallas kernels, on_band(): pl.pallas_call(network_kernel, out_shape=(jax.ShapeDtypeStruct((2,) + ban...  409 us

profile of v1, /device:TPU:0, one launch (start us, length us, event | category | flops | bytes accessed | tf_op | source)
XLA Modules:
  0.0 430.1 jit_solution(3126843494523114178)
XLA Ops:
  0.6 408.9 %network.1 = (bf16[2,8,128,512]{3,2,1,0:T(8,128)(2,1)}, bf16[2,8,128,512]{3,2,1,0:T(8,128)(2,1)}, bf16[4,8704,128]{2,1,0:T(8,128)(2,1)}, bf16[4,2048,128]{2,1,0:...) custom-call(bf16[2,8,128,512]{3,2,1,0:T(8,128)(2,1)} %bitcast.51, ...), custom_call_target="tpu_custom_call" | custom-call | tf_op jit(solution)/shard_map/network/pallas_call | solution.py:1688
  409.5 1.2 fusion.2
  410.7 1.2 fusion.4
  411.9 0.9 fusion.1
  412.7 0.9 convert_bitcast_fusion
  413.6 1.1 fusion
  414.7 1.6 slice.59
  416.3 1.8 fusion.3
  418.0 0.2 pad_maximum_fusion
  418.3 1.1 convert.14
  419.4 2.2 convert.15
  421.6 0.0 copy-start
  421.6 2.2 convert.16
  423.8 0.0 copy-done
  423.8 0.0 copy-start.1
  423.8 2.6 bitcast_convert_fusion
  426.3 0.0 copy-done.1
  426.3 0.0 copy-start.5
  426.3 0.0 copy-start.4
  426.3 0.0 copy-start.3
  426.4 0.0 copy-start.2
  426.4 1.3 copy.32
  427.7 0.0 copy-done.5
  427.7 0.6 copy.33
  428.3 0.0 copy-done.4
  428.3 0.6 copy.34
  428.9 0.0 copy-done.3
  428.9 0.6 copy.35
  429.5 0.0 copy-done.2
  429.5 0.6 copy.36
Async XLA Ops:
  421.6 2.2 copy-start
  423.8 2.6 copy-start.1
  426.3 1.3 copy-start.5
  426.3 1.9 copy-start.4
  426.3 2.5 copy-start.3
  426.4 3.1 copy-start.2

commit v2 on v1

--- a/solution.py
+++ b/solution.py
@@ -600,7 +600,6 @@
     me = jnp.where(s == 0, d, mirrored(d))
     first = (me == 0).astype(F32)
     at_z = lax.div(d, 4)
-    outer = (at_z == 0) | (at_z == 3)
 
     def member(group, k):
         core = differ(lax.div(k, per), group)
@@ -670,19 +669,8 @@
     def push_rows(parity, window, do):
         if window % 2:
             row = 4 * parity + window - 1
-
-            @pl.when(jnp.logical_not(outer))
-            def _():
-                do(row)
-                do(row + 1)
-        else:
-            index = 3 * parity + window // 2
-            row = jnp.where(index < 4, index, 2 * index - 4)
-
-            @pl.when(outer)
-            def _():
-                do(row)
-                pl.when(index >= 4)(lambda: do(row + 1))
+            do(row)
+            do(row + 1)
 
     pl.when(stays)(lambda: input_near().start())
     when_far(lambda: input_far(0).start())

time: 432 us -> 425 us (0.984)
  Pallas kernels: 409 us -> 403 us
    pallas_call x1, Pallas kernels: 409 us -> 403 us  [on_band(): pl.pallas_call(network_kernel, out_shape=(jax.ShapeDtypeStruct((2,) + ban...]
where the time goes in v2:
time: 425 us; the launch traced here: 424 us
  Pallas kernels  403 us (95%)
  other arithmetic  11.1 us (3%)
  local copies, waits for them, and re-layouts  9.45 us (2%)
    pallas_call x1, Pallas kernels, on_band(): pl.pallas_call(network_kernel, out_shape=(jax.ShapeDtypeStruct((2,) + ban...  403 us

profile of v2, /device:TPU:0, one launch (start us, length us, event | category | flops | bytes accessed | tf_op | source)
XLA Modules:
  0.0 423.9 jit_solution(10044944805607038609)
XLA Ops:
  0.6 402.7 %network.1 = (bf16[2,8,128,512]{3,2,1,0:T(8,128)(2,1)}, bf16[2,8,128,512]{3,2,1,0:T(8,128)(2,1)}, bf16[4,8704,128]{2,1,0:T(8,128)(2,1)}, bf16[4,2048,128]{2,1,0:...) custom-call(bf16[2,8,128,512]{3,2,1,0:T(8,128)(2,1)} %bitcast.51, ...), custom_call_target="tpu_custom_call" | custom-call | tf_op jit(solution)/shard_map/network/pallas_call | solution.py:1676
  403.4 1.2 fusion.2
  404.5 1.2 fusion.4
  405.7 0.9 fusion.1
  406.6 0.9 convert_bitcast_fusion
  407.4 1.1 fusion
  408.5 1.6 slice.59
  410.1 1.8 fusion.3
  411.9 0.2 pad_maximum_fusion
  412.1 1.1 convert.14
  413.2 2.2 convert.15
  415.4 0.0 copy-start
  415.4 2.2 convert.16
  417.6 0.0 copy-done
  417.6 0.0 copy-start.1
  417.6 2.6 bitcast_convert_fusion
  420.2 0.0 copy-done.1
  420.2 0.0 copy-start.5
  420.2 0.0 copy-start.4
  420.2 0.0 copy-start.3
  420.2 0.0 copy-start.2
  420.2 1.3 copy.32
  421.5 0.0 copy-done.5
  421.5 0.6 copy.33
  422.1 0.0 copy-done.4
  422.1 0.6 copy.34
  422.7 0.0 copy-done.3
  422.7 0.6 copy.35
  423.3 0.0 copy-done.2
  423.3 0.6 copy.36
Async XLA Ops:
  415.4 2.2 copy-start
  417.6 2.6 copy-start.1
  420.2 1.3 copy-start.5
  420.2 1.9 copy-start.4
  420.2 2.5 copy-start.3
  420.2 3.1 copy-start.2
